TPU v7x, 32 devices: a whole 2x2x4 slice. The times are simulated.
32 devices in a mesh: prow: 4 (over x, core), pcol: 8 (over z, y).
Axes of the slice: x: 2, y: 2, z: 4, core: 2. Of those that a mesh axis runs over, the one named last changes fastest.
Arguments:
- diag_block: float32 [512, 512], P('prow'), as said below
- panel_cols: float32 [8192, 512], P(('prow', 'pcol')), may hold values from -3 to 3
- trailing: float32 [8192, 8192], P('prow', 'pcol'), may hold values from -6 to 6
- geno_top: float32 [512, 2048], P('prow', 'pcol'), may hold values from -6 to 6
- geno_rest: float32 [8192, 2048], P('prow', 'pcol'), may hold values from -6 to 6
- pheno_top: float32 [512], P('prow'), may hold values from -6 to 6
- pheno_rest: float32 [8192], P('prow'), may hold values from -6 to 6
Outputs:
- updated_block: float32 [8192, 8192], P('prow', 'pcol')
- panel_factor: float32 [8192, 512], P(('prow', 'pcol'))
- white_geno: float32 [8192, 2048], P('prow', 'pcol')
- score_stat: float32 [2048], P('pcol')
- info_stat: float32 [2048], P('pcol')
Inputs may be any that keep to these rules, and one draw needn't show every extreme that they name: diag_block is symmetric and positive definite; its diagonal entries lie between 3 and 4.5 and its off-diagonal entries have magnitude at most 0.8.
All inputs are finite; a program needn't handle non-finite values.
Results may differ from a plain program's by a relative error of at most 0.000096.
Values sent between devices are 32-bit elements; how exact they have to be, the bound alone decides.
A program may use at most 64 MiB of HBM per device.

v0:
```python
import functools

import jax
import jax.numpy as jnp
from jax import lax
from jax.experimental import pallas as pl
from jax.experimental.pallas import tpu as pltpu
from jax.sharding import PartitionSpec as P

MESH = pl.DeviceIdType.MESH
HIGHEST = lax.Precision.HIGHEST
TILE = 8
BLOCK = 128


def split3(value):
    hi = value.astype(jnp.bfloat16).astype(jnp.float32)
    rest = value - hi
    mid = rest.astype(jnp.bfloat16).astype(jnp.float32)
    return hi, mid, rest - mid


def tile_step(m_ref, step):
    start = pl.multiple_of(step * TILE, TILE)
    left = m_ref[pl.ds(start, TILE), :BLOCK]
    right = m_ref[pl.ds(start, TILE), BLOCK:]
    rolled = pltpu.roll(left, lax.rem(BLOCK - start, BLOCK), 1)
    cols = [jnp.broadcast_to(rolled[:, k : k + 1], (TILE, BLOCK)) for k in range(TILE)]
    rows = lax.broadcasted_iota(jnp.int32, (TILE, BLOCK), 0)
    lanes = lax.broadcasted_iota(jnp.int32, (TILE, BLOCK), 1)
    for j in range(TILE):
        inv = lax.rsqrt(jnp.broadcast_to(cols[j][j : j + 1, :], (TILE, BLOCK)))
        factor = jnp.where(rows > j, cols[j] * inv, 0.0)

        def work(value):
            scaled = jnp.broadcast_to(value[j : j + 1, :], (TILE, BLOCK)) * inv
            return jnp.where(rows == j, scaled, value - factor * scaled)

        left, right = work(left), work(right)
        for k in range(j + 1, TILE):
            cols[k] = work(cols[k])
    m_ref[pl.ds(start, TILE), :BLOCK] = left
    m_ref[pl.ds(start, TILE), BLOCK:] = right
    both = jnp.concatenate([left, right], axis=1)
    mult = jnp.where(lanes >= start + TILE, left, 0.0)
    a0, a1, a2 = split3(mult)
    b0, b1, b2 = split3(both)
    lhs = jnp.concatenate([a0, a0, a1, a0, a1, a2], axis=0).astype(jnp.bfloat16)
    rhs = jnp.concatenate([b0, b1, b0, b2, b1, b0], axis=0).astype(jnp.bfloat16)
    m_ref[...] -= lax.dot_general(
        lhs, rhs, (((0,), (0,)), ((), ())), preferred_element_type=jnp.float32
    )


def dot_t(a, b):
    return lax.dot_general(
        a, b, (((0,), (0,)), ((), ())), precision=HIGHEST, preferred_element_type=jnp.float32
    )


def dot_n(a, b):
    return jnp.dot(a, b, precision=HIGHEST, preferred_element_type=jnp.float32)


def invert(a_ref, w_ref, m_ref, events):
    width = a_ref.shape[0]
    blocks = width // BLOCK
    tiles = BLOCK // TILE
    w_ref[...] = jnp.zeros_like(w_ref)
    eye = (
        lax.broadcasted_iota(jnp.int32, (BLOCK, BLOCK), 0)
        == lax.broadcasted_iota(jnp.int32, (BLOCK, BLOCK), 1)
    ).astype(jnp.float32)
    slot = 0
    for k in range(blocks):
        lo, hi = k * BLOCK, (k + 1) * BLOCK
        m_ref[:, :BLOCK] = a_ref[lo:hi, lo:hi]
        m_ref[:, BLOCK:] = eye
        for part in range(2):

            def body(step, carry):
                tile_step(m_ref, step)
                return carry

            lax.fori_loop(part * tiles // 2, (part + 1) * tiles // 2, body, 0)
            if part == 0:
                if slot < len(events):
                    events[slot]()
                slot += 1
        own = m_ref[:, BLOCK:]
        if k > 0:
            w_ref[lo:hi, :lo] = dot_n(own, w_ref[lo:hi, :lo])
        w_ref[lo:hi, lo:hi] = own
        if k < blocks - 1:
            upper = dot_n(own, a_ref[lo:hi, hi:])
            a_ref[hi:, hi:] -= dot_t(upper, upper)
            w_ref[hi:, :hi] -= dot_t(upper, w_ref[lo:hi, :hi])
        if slot < len(events):
            events[slot]()
        slot += 1
    while slot < len(events):
        events[slot]()
        slot += 1


def gather_kernel(
    ly, lz, group,
    diag_in, top_in, panel_in,
    w_out, row_out, col_out, top_out,
    a_ref, m_ref,
    barrier_free, small_send, small_recv, row_send, row_recv, col_send, col_recv, local_sem,
):
    r, c = lax.axis_index("prow"), lax.axis_index("pcol")
    z, y = c // ly, lax.rem(c, ly)
    sib = r + 1 - 2 * lax.rem(r, 2)
    cross = r + 2 - 4 * (r // 2)
    diag_x = sib + 2 - 4 * (sib // 2)
    other = z * ly + (1 - y)
    col_parts = col_out.shape[0]
    root = c // group
    first = lax.rem(c, group) * col_parts
    is_root = root == r
    root_sib = root + 1 - 2 * lax.rem(root, 2)
    root_cross = root + 2 - 4 * (root // 2)
    del barrier_free

    barrier = pltpu.get_barrier_semaphore()

    def greet(row, col):
        pl.semaphore_signal(barrier, inc=1, device_id={"prow": row, "pcol": col}, device_id_type=MESH)

    greet(sib, c)
    greet(cross, c)
    greet(r, other)

    @pl.when(z > 0)
    def _():
        greet(r, c - ly)

    @pl.when(z < lz - 1)
    def _():
        greet(r, c + ly)

    pl.semaphore_wait(barrier, 3 + jnp.minimum(z, 1) + jnp.minimum(lz - 1 - z, 1))

    def remote(src, dst, send, recv, row, col):
        return pltpu.make_async_remote_copy(
            src_ref=src, dst_ref=dst, send_sem=send, recv_sem=recv,
            device_id={"prow": row, "pcol": col}, device_id_type=MESH,
        )

    height = diag_in.shape[0]

    def diag_at(q):
        return a_ref.at[pl.ds(pl.multiple_of(q * height, height), height), :]

    def small(kind, lane):
        source = diag_in if kind == 0 else top_in
        place = diag_at if kind == 0 else (lambda q: top_out.at[q])
        part = cross if lane == 2 else r
        src = place(part) if lane == 2 else source
        return remote(
            src, place(part), small_send.at[kind, lane], small_recv.at[kind, part],
            cross if lane == 1 else sib, c,
        )

    def small_wait(kind, part):
        place = diag_at if kind == 0 else (lambda q: top_out.at[q])
        remote(place(part), place(part), small_send.at[kind, 0], small_recv.at[kind, part], sib, c).wait_recv()

    def row_copy(way, b, own):
        target = (c + ly, c - ly, other)[way]
        return remote(
            panel_in if own else row_out.at[b], row_out.at[b],
            row_send.at[way, b], row_recv.at[b], r, target,
        )

    def row_wait(b):
        remote(row_out.at[b], row_out.at[b], row_send.at[0, b], row_recv.at[b], r, other).wait_recv()

    def col_copies(b, own):
        i = b - first
        src = panel_in if own else row_out.at[b]
        return (
            remote(src, col_out.at[i], col_send.at[0, i], col_recv.at[i], cross, c),
            remote(src, col_out.at[i], col_send.at[1, i], col_recv.at[i], sib, c),
            pltpu.make_async_copy(src, col_out.at[i], local_sem.at[1 + i]),
        )

    def in_col(b):
        return is_root & (b >= first) & (b < first + col_parts)

    def col_start(b, own):
        @pl.when(in_col(b))
        def _():
            for copy in col_copies(b, own):
                copy.start()

    def col_finish(b, own):
        @pl.when(in_col(b))
        def _():
            one, two, three = col_copies(b, own)
            one.wait_send()
            two.wait_send()
            three.wait()

    def up(fn):
        pl.when(z < lz - 1)(fn)

    def down(fn):
        pl.when(z > 0)(fn)

    small(0, 1).start()
    small(0, 0).start()
    row_copy(2, c, True).start()
    up(lambda: row_copy(0, c, True).start())
    down(lambda: row_copy(1, c, True).start())
    small(1, 1).start()
    small(1, 0).start()
    own_copy = pltpu.make_async_copy(panel_in, row_out.at[c], local_sem.at[0])
    own_copy.start()
    top_copy = pltpu.make_async_copy(top_in, top_out.at[r], local_sem.at[1 + col_parts])
    top_copy.start()
    col_start(c, True)
    a_ref[pl.ds(pl.multiple_of(r * height, height), height), :] = diag_in[...]
    small_wait(0, cross)
    small(0, 2).start()
    small_wait(0, sib)
    small_wait(0, diag_x)
    small(0, 2).wait_send()

    def hop(d):
        low, high = c - d * ly, c + d * ly

        @pl.when(z >= d)
        def _():
            row_wait(low)
            up(lambda: row_copy(0, low, False).start())
            row_copy(2, low, False).start()
            col_start(low, False)

        @pl.when(z + d < lz)
        def _():
            row_wait(high)
            down(lambda: row_copy(1, high, False).start())
            row_copy(2, high, False).start()
            col_start(high, False)

    def across(d):
        def one(b):
            row_wait(b)
            col_start(b, False)

        if d == 0:
            one(other)
        else:
            pl.when(z >= d)(lambda: one(other - d * ly))
            pl.when(z + d < lz)(lambda: one(other + d * ly))

    def top_event():
        small_wait(1, cross)
        small(1, 2).start()

    def first_event():
        hop(1)
        across(0)

    def make(d):
        def run():
            if d < lz:
                hop(d)
            across(d - 1)

        return run

    def nothing():
        pass

    events = [first_event, top_event, make(2), nothing, make(3), nothing, nothing]
    events += [make(d) for d in range(4, lz + 1)]
    invert(a_ref, w_out, m_ref, events)

    def handed(i):
        return remote(col_out.at[i], col_out.at[i], col_send.at[1, i], col_recv.at[i], sib, c)

    @pl.when(r == root_cross)
    def _():
        for i in range(col_parts):
            handed(i).wait_recv()
            handed(i).start()
        for i in range(col_parts):
            handed(i).wait_send()

    @pl.when(jnp.logical_not(is_root) & (r != root_cross))
    def _():
        for i in range(col_parts):
            handed(i).wait_recv()

    del root_sib
    small(0, 1).wait_send()
    small(0, 0).wait_send()
    small(1, 1).wait_send()
    small(1, 0).wait_send()
    small(1, 2).wait_send()
    small_wait(1, sib)
    small_wait(1, diag_x)
    own_copy.wait()
    top_copy.wait()
    row_copy(2, c, True).wait_send()
    up(lambda: row_copy(0, c, True).wait_send())
    down(lambda: row_copy(1, c, True).wait_send())
    col_finish(c, True)
    col_finish(other, False)
    for d in range(1, lz):

        @pl.when(z >= d)
        def _():
            low = c - d * ly
            up(lambda: row_copy(0, low, False).wait_send())
            row_copy(2, low, False).wait_send()
            col_finish(low, False)
            col_finish(other - d * ly, False)

        @pl.when(z + d < lz)
        def _():
            high = c + d * ly
            down(lambda: row_copy(1, high, False).wait_send())
            row_copy(2, high, False).wait_send()
            col_finish(high, False)
            col_finish(other + d * ly, False)


def gather_and_invert(diag_block, top_aug, panel_cols, prow_size, pcol_size):
    ly = 2
    lz = pcol_size // ly
    height, width = diag_block.shape
    rows_piece = panel_cols.shape[0]
    col_parts = prow_size
    any_spec = pl.BlockSpec(memory_space=pl.ANY)
    vmem = pl.BlockSpec(memory_space=pltpu.VMEM)
    dma = pltpu.SemaphoreType.DMA
    f32 = jnp.float32
    return pl.pallas_call(
        functools.partial(gather_kernel, ly, lz, pcol_size // prow_size),
        out_shape=(
            jax.ShapeDtypeStruct((width, width), f32),
            jax.ShapeDtypeStruct((pcol_size, rows_piece, width), f32),
            jax.ShapeDtypeStruct((col_parts, rows_piece, width), f32),
            jax.ShapeDtypeStruct((prow_size,) + top_aug.shape, f32),
        ),
        in_specs=[vmem, any_spec, any_spec],
        out_specs=(vmem, any_spec, any_spec, any_spec),
        scratch_shapes=[
            pltpu.VMEM((width, width), f32),
            pltpu.VMEM((BLOCK, 2 * BLOCK), f32),
            pltpu.SemaphoreType.REGULAR,
            dma((2, 3)),
            dma((2, prow_size)),
            dma((3, pcol_size)),
            dma((pcol_size,)),
            dma((2, col_parts)),
            dma((col_parts,)),
            dma((2 + col_parts,)),
        ],
        compiler_params=pltpu.CompilerParams(
            collective_id=0, has_side_effects=True, vmem_limit_bytes=24 * 1024 * 1024
        ),
    )(diag_block, top_aug, panel_cols)


def dot3(a, b, dims):
    return lax.dot_general(a, b, (dims, ((), ())), precision=lax.Precision.HIGH)


def local(diag_block, panel_cols, trailing, geno_top, geno_rest, pheno_top, pheno_rest):
    prow_size, pcol_size = lax.axis_size("prow"), lax.axis_size("pcol")
    height, width = diag_block.shape
    rows_piece = panel_cols.shape[0]
    row_count = rows_piece * pcol_size
    variants = geno_top.shape[1]
    pad = jnp.broadcast_to(pheno_top[:, None], (height, BLOCK))
    top_aug = jnp.concatenate([geno_top, pad], axis=1)
    inverse, whole, col_raw, top_all = gather_and_invert(
        diag_block, top_aug, panel_cols, prow_size, pcol_size
    )
    whole = whole.reshape(row_count, width)
    col_raw = col_raw.reshape(-1, width)
    top_all = top_all.reshape(width, variants + BLOCK)
    white_aug = dot3(inverse, top_all, ((1,), (0,)))
    panel_rows = dot3(whole, inverse, ((1,), (1,)))
    col_panel = dot3(col_raw, inverse, ((1,), (1,)))
    own_factor = lax.dynamic_slice_in_dim(
        panel_rows, lax.axis_index("pcol") * rows_piece, rows_piece, 0
    )
    top_white, pheno_white_top = white_aug[:, :variants], white_aug[:, variants]
    shift = dot3(panel_rows, white_aug, ((1,), (0,)))
    white_geno = geno_rest - shift[:, :variants]
    pheno_white = pheno_rest - shift[:, variants]
    part_score = jnp.dot(pheno_white, white_geno, precision=HIGHEST)
    part_info = jnp.sum(white_geno * white_geno, axis=0)
    score_sum, info_sum = lax.psum((part_score, part_info), "prow")
    updated_block = trailing - dot3(panel_rows, col_panel, ((1,), (1,)))
    count = width + row_count * prow_size
    score_stat = (score_sum + jnp.dot(pheno_white_top, top_white, precision=HIGHEST)) / jnp.sqrt(
        jnp.float32(count)
    )
    info_stat = (info_sum + jnp.sum(top_white * top_white, axis=0)) / jnp.float32(count)
    return (updated_block, own_factor, white_geno, score_stat, info_stat)


def solution(mesh):
    placed = (
        P("prow", None),
        P(("prow", "pcol"), None),
        P("prow", "pcol"),
        P("prow", "pcol"),
        P("prow", "pcol"),
        P("prow"),
        P("prow"),
    )
    return jax.shard_map(
        local,
        mesh=mesh,
        in_specs=placed,
        out_specs=(
            P("prow", "pcol"),
            P(("prow", "pcol"), None),
            P("prow", "pcol"),
            P("pcol"),
            P("pcol"),
        ),
        check_vma=False,
    )
```

profile of v0, /device:TPU:18, one launch (start us, length us, event | category | flops | bytes accessed | tf_op | source)
XLA Modules:
  0.0 119.7 jit_solution(1351733767857107481)
XLA Ops:
  0.6 0.7 broadcast_in_dim.2
  1.4 0.9 pad_maximum_fusion.top_in
  2.3 0.0 copy-start
  2.3 1.0 copy-done
  3.3 0.0 copy-start.1
  3.3 0.9 copy-done.1
  4.3 63.6 %shard_map.110 = (f32[512,512]{1,0:T(8,128)S(1)}, f32[8,256,512]{2,1,0:T(8,128)S(1)}, f32[4,256,512]{2,1,0:T(8,128)S(1)}, f32[4,128,384]{2,1,0:T(8,128)S(1)}) custom-call(f32[128,512]{1,0:T(8,128)S(1)} %copy-done.1, f32[128,384]{1,0:T(8,128)S(1)} %pad_maximum_fusion.top_in, f32[256,512]{1,0:T(8,128)S(1)} %copy-done), custom_call_target="tpu_custom_call" | custom-call | tf_op jit(solution)/shard_map/pallas_call | solution.py:343
  67.9 0.8 fusion.5
  68.8 0.0 copy-start.5
  68.8 3.7 %fusion.3 = f32[2048,512]{1,0:T(8,128)S(1)} fusion(f32[2048,512]{1,0:T(8,128)S(1)} %bitcast.20, f32[512,512]{1,0:T(8,128)S(1)} %get-tuple-element.10), kind=kOutput, calls=%fused_computation.11 | convolution fusion | flops 3221225472 | bytes 9437184 | tf_op jit(solution)/shard_map/dot_general | solution.py:372
  72.5 0.0 copy-done.5
  72.5 0.0 copy-start.2
  72.5 1.9 %copy-done.2 = f32[2048,512]{1,0:T(8,128)} copy-done((f32[2048,512]{1,0:T(8,128)}, f32[2048,512]{1,0:T(8,128)S(1)}, u32[]{:S(2)}) %copy-start.2) | copy-done | bytes 4194328
  74.5 4.4 %fusion.6 = f32[2048,384]{0,1:T(8,128)} fusion(f32[2048,512]{1,0:T(8,128)S(1)} %fusion.3, f32[512,384]{0,1:T(8,128)S(1)} %fusion.5), kind=kOutput, calls=%fused_computation.14 | convolution fusion | flops 2415919104 | bytes 8126464 | tf_op jit(solution)/shard_map/dot_general | solution.py:372
  78.8 2.9 %copy.12 = f32[2048,256]{0,1:T(8,128)} copy(f32[2048,256]{1,0:T(8,128)} %param.11) | data formatting | bytes 4194304 | tf_op args[4]
  81.7 0.0 slice-start
  81.7 0.0 copy-start.6
  81.7 2.6 %multiply_reduce_fusion = (f32[256]{0:T(256)S(1)}, f32[2048,256]{0,1:T(8,128)S(1)}) fusion(f32[2048,256]{0,1:T(8,128)} %copy.12, f32[2048,384]{0,1:T(8,128)} %fusion.6), kind=kLoop, calls=%fused_computation.2 | loop fusion | flops 1572608 | bytes 6292480 | tf_op jit(solution)/shard_map/reduce_sum | solution.py:400
  84.3 0.0 copy-start.4
  84.3 0.0 slice-done
  84.3 0.0 copy-done.6
  84.3 1.3 %copy-done.4 = f32[2048,256]{0,1:T(8,128)} copy-done((f32[2048,256]{0,1:T(8,128)}, f32[2048,256]{0,1:T(8,128)S(1)}, u32[]{:S(2)}) %copy-start.4) | copy-done | bytes 2097176
  85.6 1.7 %fusion.7 = f32[1,256]{1,0:T(1,128)S(1)} fusion(f32[2048,1]{0,1:T(1,128)S(1)} %bitcast.24, f32[2048,256]{0,1:T(8,128)S(1)} %get-tuple-element.21), kind=kOutput, calls=%fused_computation.15 | convolution fusion | flops 6291456 | bytes 2106368 | tf_op jit(solution)/shard_map/dot_general | solution.py:399
  87.3 11.0 %all-reduce = (f32[256]{0:T(256)S(1)}, f32[256]{0:T(256)S(1)}) all-reduce(f32[256]{0:T(256)S(1)} %bitcast.25, f32[256]{0:T(256)S(1)} %get-tuple-element.20), channel_id=1, replica_groups=mesh['prow'=4,'pcol'=8] {'prow'}, use_global_device_ids=true, to_apply=%region_0.0 | all-reduce | flops 512 | bytes 4096 | tf_op jit(solution)/shard_map/psum | solution.py:401
  98.4 1.6 %fusion = f32[1,256]{1,0:T(1,128)S(1)} fusion(f32[512,384]{0,1:T(8,128)} %copy-done.5), kind=kOutput, calls=%fused_computation.4 | convolution fusion | flops 1572864 | bytes 527360 | tf_op jit(solution)/shard_map/dot_general | solution.py:404
  99.9 1.2 multiply_reduce_fusion.1
  101.1 0.6 add_multiply_fusion
  101.7 2.9 %copy.13 = f32[2048,256]{1,0:T(8,128)} copy(f32[2048,256]{0,1:T(8,128)} %copy-done.4) | data formatting | bytes 4194304
  104.6 0.0 copy-start.3
  104.6 1.8 %fusion.4 = f32[1024,512]{1,0:T(8,128)S(1)} fusion(f32[1024,512]{1,0:T(8,128)S(1)} %bitcast.21, f32[512,512]{1,0:T(8,128)S(1)} %get-tuple-element.10), kind=kOutput, calls=%fused_computation.12 | convolution fusion | flops 1610612736 | bytes 5242880 | tf_op jit(solution)/shard_map/dot_general | solution.py:372
  106.4 0.3 copy-done.3
  106.8 11.1 %convolution_subtract_fusion = f32[2048,1024]{1,0:T(8,128)} fusion(f32[2048,1024]{1,0:T(8,128)} %param.9, f32[2048,512]{1,0:T(8,128)S(1)} %copy-done.3, f32[1024,512]{1,0:T(8,128)S(1)} %fusion.4), kind=kOutput, calls=%fused_computation | convolution fusion | flops 6444548096 | bytes 23068672 | tf_op jit(solution)/shard_map/dot_general | solution.py:372
  117.8 1.9 %constant_dynamic-slice_fusion = f32[256,512]{1,0:T(8,128)} fusion(f32[2048,512]{1,0:T(8,128)} %copy-done.2, s32[]{:T(128)S(6)} %select_n.3), kind=kLoop, calls=%fused_computation.10 | loop fusion | bytes 1048580 | tf_op jit(solution)/shard_map/dynamic_slice | solution.py:392
  (1 shorter events, 0.0 us)
Async XLA Ops:
  2.3 1.0 copy-start
  3.3 0.9 copy-start.1
  68.8 3.7 %copy-start.5 = (f32[512,384]{0,1:T(8,128)}, f32[512,384]{0,1:T(8,128)S(1)}, u32[]{:S(2)}) copy-start(f32[512,384]{0,1:T(8,128)S(1)} %fusion.5) | copy-start | bytes 2359300
  72.5 1.9 %copy-start.2 = (f32[2048,512]{1,0:T(8,128)}, f32[2048,512]{1,0:T(8,128)S(1)}, u32[]{:S(2)}) copy-start(f32[2048,512]{1,0:T(8,128)S(1)} %fusion.3) | copy-start | bytes 12582916
  81.7 2.6 %slice-start = ((f32[2048,384]{0,1:T(8,128)}), f32[2048,1]{0,1:T(1,128)S(1)}, s32[]{:S(2)}) async-start(f32[2048,384]{0,1:T(8,128)} %fusion.6), calls=%async_computation | async-start | bytes 16384 | tf_op jit(solution)/shard_map/slice | solution.py:398
  81.7 2.6 %copy-start.6 = (f32[2048]{0:T(1024)S(1)}, f32[2048]{0:T(1024)}, u32[]{:S(2)}) copy-start(f32[2048]{0:T(1024)} %param.13) | copy-start | bytes 24580
  84.3 1.3 %copy-start.4 = (f32[2048,256]{0,1:T(8,128)}, f32[2048,256]{0,1:T(8,128)S(1)}, u32[]{:S(2)}) copy-start(f32[2048,256]{0,1:T(8,128)S(1)} %get-tuple-element.21) | copy-start | bytes 6291460
  104.6 2.2 %copy-start.3 = (f32[2048,512]{1,0:T(8,128)S(1)}, f32[2048,512]{1,0:T(8,128)}, u32[]{:S(2)}) copy-start(f32[2048,512]{1,0:T(8,128)} %copy-done.2) | copy-start | bytes 12582916
where the time goes:
time: 120 us
  Pallas kernels  63.6 us (53%)
  matrix products  25.1 us (21%)
  local copies, waits for them, and re-layouts  13.9 us (12%)
  blocking collectives  11 us (9%)
  other arithmetic  5.24 us (4%)
    pallas_call x1, Pallas kernels, gather_and_invert(): pl.pallas_call(functools.partial(gather_kernel, ly, lz, pcol_size // prow...  63.6 us
    dot_general x5, matrix products, dot3(): return lax.dot_general(a, b, (dims, ((), ())), precision=lax.Precision.HIGH)  21.9 us
    unnamed x16, local copies, waits for them, and re-layouts  11.3 us
    psum x1, blocking collectives, local(): score_sum, info_sum = lax.psum((part_score, part_info), 'prow')  11 us
    reduce_sum x1, other arithmetic, local(): part_info = jnp.sum(white_geno * white_geno, axis=0)  2.56 us

commit v1 on v0

--- a/solution.py
+++ b/solution.py
@@ -29,7 +29,9 @@
     rows = lax.broadcasted_iota(jnp.int32, (TILE, BLOCK), 0)
     lanes = lax.broadcasted_iota(jnp.int32, (TILE, BLOCK), 1)
     for j in range(TILE):
-        inv = lax.rsqrt(jnp.broadcast_to(cols[j][j : j + 1, :], (TILE, BLOCK)))
+        pivot = jnp.broadcast_to(cols[j][j : j + 1, :], (TILE, BLOCK))
+        inv = lax.rsqrt(pivot)
+        inv = inv * (1.5 - (0.5 * pivot) * inv * inv)
         factor = jnp.where(rows > j, cols[j] * inv, 0.0)
 
         def work(value):
@@ -105,10 +107,10 @@
 
 def gather_kernel(
     ly, lz, group,
-    diag_in, top_in, panel_in,
-    w_out, row_out, col_out, top_out,
+    diag_in, top_in, pheno_in, panel_in,
+    w_out, row_out, col_out, top_out, pheno_out,
     a_ref, m_ref,
-    barrier_free, small_send, small_recv, row_send, row_recv, col_send, col_recv, local_sem,
+    small_send, small_recv, row_send, row_recv, col_send, col_recv, local_sem,
 ):
     r, c = lax.axis_index("prow"), lax.axis_index("pcol")
     z, y = c // ly, lax.rem(c, ly)
@@ -120,9 +122,7 @@
     root = c // group
     first = lax.rem(c, group) * col_parts
     is_root = root == r
-    root_sib = root + 1 - 2 * lax.rem(root, 2)
     root_cross = root + 2 - 4 * (root // 2)
-    del barrier_free
 
     barrier = pltpu.get_barrier_semaphore()
 
@@ -154,9 +154,11 @@
     def diag_at(q):
         return a_ref.at[pl.ds(pl.multiple_of(q * height, height), height), :]
 
+    places = (diag_at, lambda q: top_out.at[q], lambda q: pheno_out.at[q])
+
     def small(kind, lane):
-        source = diag_in if kind == 0 else top_in
-        place = diag_at if kind == 0 else (lambda q: top_out.at[q])
+        source = (diag_in, top_in, pheno_in)[kind]
+        place = places[kind]
         part = cross if lane == 2 else r
         src = place(part) if lane == 2 else source
         return remote(
@@ -165,7 +167,7 @@
         )
 
     def small_wait(kind, part):
-        place = diag_at if kind == 0 else (lambda q: top_out.at[q])
+        place = places[kind]
         remote(place(part), place(part), small_send.at[kind, 0], small_recv.at[kind, part], sib, c).wait_recv()
 
     def row_copy(way, b, own):
@@ -215,18 +217,23 @@
     row_copy(2, c, True).start()
     up(lambda: row_copy(0, c, True).start())
     down(lambda: row_copy(1, c, True).start())
-    small(1, 1).start()
-    small(1, 0).start()
+    for kind in (1, 2):
+        small(kind, 1).start()
+        small(kind, 0).start()
     own_copy = pltpu.make_async_copy(panel_in, row_out.at[c], local_sem.at[0])
     own_copy.start()
     top_copy = pltpu.make_async_copy(top_in, top_out.at[r], local_sem.at[1 + col_parts])
     top_copy.start()
+    pheno_copy = pltpu.make_async_copy(pheno_in, pheno_out.at[r], local_sem.at[2 + col_parts])
+    pheno_copy.start()
+    diag_copy = pltpu.make_async_copy(diag_in, diag_at(r), local_sem.at[3 + col_parts])
+    diag_copy.start()
     col_start(c, True)
-    a_ref[pl.ds(pl.multiple_of(r * height, height), height), :] = diag_in[...]
     small_wait(0, cross)
     small(0, 2).start()
     small_wait(0, sib)
     small_wait(0, diag_x)
+    diag_copy.wait()
     small(0, 2).wait_send()
 
     def hop(d):
@@ -258,8 +265,9 @@
             pl.when(z + d < lz)(lambda: one(other + d * ly))
 
     def top_event():
-        small_wait(1, cross)
-        small(1, 2).start()
+        for kind in (1, 2):
+            small_wait(kind, cross)
+            small(kind, 2).start()
 
     def first_event():
         hop(1)
@@ -296,16 +304,16 @@
         for i in range(col_parts):
             handed(i).wait_recv()
 
-    del root_sib
     small(0, 1).wait_send()
     small(0, 0).wait_send()
-    small(1, 1).wait_send()
-    small(1, 0).wait_send()
-    small(1, 2).wait_send()
-    small_wait(1, sib)
-    small_wait(1, diag_x)
+    for kind in (1, 2):
+        for lane in range(3):
+            small(kind, lane).wait_send()
+        small_wait(kind, sib)
+        small_wait(kind, diag_x)
     own_copy.wait()
     top_copy.wait()
+    pheno_copy.wait()
     row_copy(2, c, True).wait_send()
     up(lambda: row_copy(0, c, True).wait_send())
     down(lambda: row_copy(1, c, True).wait_send())
@@ -330,7 +338,7 @@
             col_finish(other + d * ly, False)
 
 
-def gather_and_invert(diag_block, top_aug, panel_cols, prow_size, pcol_size):
+def gather_and_invert(diag_block, geno_top, pheno_row, panel_cols, prow_size, pcol_size):
     ly = 2
     lz = pcol_size // ly
     height, width = diag_block.shape
@@ -346,30 +354,174 @@
             jax.ShapeDtypeStruct((width, width), f32),
             jax.ShapeDtypeStruct((pcol_size, rows_piece, width), f32),
             jax.ShapeDtypeStruct((col_parts, rows_piece, width), f32),
-            jax.ShapeDtypeStruct((prow_size,) + top_aug.shape, f32),
-        ),
-        in_specs=[vmem, any_spec, any_spec],
-        out_specs=(vmem, any_spec, any_spec, any_spec),
+            jax.ShapeDtypeStruct((prow_size,) + geno_top.shape, f32),
+            jax.ShapeDtypeStruct((prow_size,) + pheno_row.shape, f32),
+        ),
+        in_specs=[any_spec] * 4,
+        out_specs=(vmem, any_spec, any_spec, any_spec, any_spec),
         scratch_shapes=[
             pltpu.VMEM((width, width), f32),
             pltpu.VMEM((BLOCK, 2 * BLOCK), f32),
-            pltpu.SemaphoreType.REGULAR,
-            dma((2, 3)),
-            dma((2, prow_size)),
+            dma((3, 3)),
+            dma((3, prow_size)),
             dma((3, pcol_size)),
             dma((pcol_size,)),
             dma((2, col_parts)),
             dma((col_parts,)),
-            dma((2 + col_parts,)),
+            dma((4 + col_parts,)),
         ],
         compiler_params=pltpu.CompilerParams(
-            collective_id=0, has_side_effects=True, vmem_limit_bytes=24 * 1024 * 1024
-        ),
-    )(diag_block, top_aug, panel_cols)
+            collective_id=0, has_side_effects=True, vmem_limit_bytes=56 * 1024 * 1024
+        ),
+    )(diag_block, geno_top, pheno_row, panel_cols)
+
+
+LAST = ((1,), (1,))
+INNER = ((1,), (0,))
+
+
+def split2(value):
+    hi = value.astype(jnp.bfloat16)
+    return hi, (value - hi.astype(jnp.float32)).astype(jnp.bfloat16)
 
 
 def dot3(a, b, dims):
-    return lax.dot_general(a, b, (dims, ((), ())), precision=lax.Precision.HIGH)
+    def one(x, y):
+        return lax.dot_general(x, y, (dims, ((), ())), preferred_element_type=jnp.float32)
+
+    return one(a[0], b[0]) + (one(a[0], b[1]) + one(a[1], b[0]))
+
+
+def whiten_kernel(
+    tile, pieces, col_tiles,
+    w_in, top_in, pheno_in, rows_in, cols_in, geno_in, rest_in,
+    hi_out, lo_out, col_hi_out, col_lo_out, own_out, geno_out, stat_out,
+    w_hi, w_lo, top_hi, top_lo, pheno_hi, pheno_lo, kept,
+):
+    step = pl.program_id(0)
+    place = lax.axis_index("pcol") * own_out.shape[0]
+
+    @pl.when(step == 0)
+    def _():
+        w_hi[...], w_lo[...] = split2(w_in[...])
+        w = (w_hi[...], w_lo[...])
+        white = dot3(w, split2(top_in[...]), INNER)
+        top_hi[...], top_lo[...] = split2(white)
+        row = jnp.broadcast_to(pheno_in[...], pheno_hi.shape)
+        pheno = split2(dot3(split2(row), w, LAST))
+        pheno_hi[...], pheno_lo[...] = pheno
+        stat_out[...] = jnp.zeros_like(stat_out)
+        stat_out[2:3, :] = dot3(pheno, (top_hi[...], top_lo[...]), INNER)[:1]
+        stat_out[3:4, :] = jnp.sum(white * white, axis=0, keepdims=True)
+
+    w = (w_hi[...], w_lo[...])
+    panel = dot3(split2(rows_in[...]), w, LAST)
+    parts = split2(panel)
+    hi_out[...], lo_out[...] = parts
+
+    @pl.when(place // tile == step)
+    def _():
+        kept[...] = panel
+        start = pl.multiple_of(lax.rem(place, tile), TILE)
+        own_out[...] = kept[pl.ds(start, own_out.shape[0]), :]
+
+    @pl.when(step < col_tiles)
+    def _():
+        col_hi_out[...], col_lo_out[...] = split2(dot3(w, split2(cols_in[...]), LAST))
+
+    white = geno_in[...] - dot3(parts, (top_hi[...], top_lo[...]), INNER)
+    geno_out[...] = white
+    pheno = rest_in[0] - dot3((pheno_hi[...], pheno_lo[...]), parts, LAST)
+    stat_out[0:1, :] += dot3(split2(pheno), split2(white), INNER)[:1]
+    stat_out[1:2, :] += jnp.sum(white * white, axis=0, keepdims=True)
+
+
+def whiten(inverse, top, pheno, rows, cols, geno_rest, pheno_rest, rows_piece):
+    width = inverse.shape[0]
+    row_count, variants = geno_rest.shape
+    col_count = cols.shape[0]
+    tile = min(256, row_count)
+    col_tile = min(256, col_count)
+    steps, col_tiles = row_count // tile, col_count // col_tile
+    f32, bf16 = jnp.float32, jnp.bfloat16
+    rest = pheno_rest.reshape(steps, 1, tile)
+
+    def fixed(shape):
+        return pl.BlockSpec(shape, lambda i: (0,) * len(shape))
+
+    def by_row(wide):
+        return pl.BlockSpec((tile, wide), lambda i: (i, 0))
+
+    last = col_tiles - 1
+    col_out = pl.BlockSpec((width, col_tile), lambda i: (0, jnp.minimum(i, last)))
+    return pl.pallas_call(
+        functools.partial(whiten_kernel, tile, rows_piece, col_tiles),
+        grid=(steps,),
+        in_specs=[
+            fixed((width, width)),
+            fixed((width, variants)),
+            fixed((1, width)),
+            by_row(width),
+            pl.BlockSpec((col_tile, width), lambda i: (jnp.minimum(i, last), 0)),
+            by_row(variants),
+            pl.BlockSpec((1, 1, tile), lambda i: (i, 0, 0)),
+        ],
+        out_specs=(
+            by_row(width), by_row(width), col_out, col_out,
+            fixed((rows_piece, width)), by_row(variants), fixed((8, variants)),
+        ),
+        out_shape=(
+            jax.ShapeDtypeStruct((row_count, width), bf16),
+            jax.ShapeDtypeStruct((row_count, width), bf16),
+            jax.ShapeDtypeStruct((width, col_count), bf16),
+            jax.ShapeDtypeStruct((width, col_count), bf16),
+            jax.ShapeDtypeStruct((rows_piece, width), f32),
+            jax.ShapeDtypeStruct((row_count, variants), f32),
+            jax.ShapeDtypeStruct((8, variants), f32),
+        ),
+        scratch_shapes=[
+            pltpu.VMEM((width, width), bf16),
+            pltpu.VMEM((width, width), bf16),
+            pltpu.VMEM((width, variants), bf16),
+            pltpu.VMEM((width, variants), bf16),
+            pltpu.VMEM((16, width), bf16),
+            pltpu.VMEM((16, width), bf16),
+            pltpu.VMEM((tile, width), f32),
+        ],
+        compiler_params=pltpu.CompilerParams(vmem_limit_bytes=40 * 1024 * 1024),
+        cost_estimate=pl.CostEstimate(
+            flops=6 * width * width * (row_count + col_count),
+            bytes_accessed=16 * 1024 * 1024,
+            transcendentals=0,
+        ),
+    )(inverse, top, pheno, rows, cols, geno_rest, rest)
+
+
+def update_kernel(hi_in, lo_in, col_hi_in, col_lo_in, trailing_in, out):
+    right = (col_hi_in[...], col_lo_in[...])
+    out[...] = trailing_in[...] - dot3((hi_in[...], lo_in[...]), right, INNER)
+
+
+def update(hi, lo, col_hi, col_lo, trailing):
+    row_count, col_count = trailing.shape
+    width = hi.shape[1]
+    tile = min(256, row_count)
+    left = pl.BlockSpec((tile, width), lambda i: (i, 0))
+    right = pl.BlockSpec((width, col_count), lambda i: (0, 0))
+    block = pl.BlockSpec((tile, col_count), lambda i: (i, 0))
+    return pl.pallas_call(
+        update_kernel,
+        grid=(row_count // tile,),
+        in_specs=[left, left, right, right, block],
+        out_specs=block,
+        out_shape=jax.ShapeDtypeStruct(trailing.shape, jnp.float32),
+        compiler_params=pltpu.CompilerParams(vmem_limit_bytes=40 * 1024 * 1024),
+        cost_estimate=pl.CostEstimate(
+            flops=6 * width * row_count * col_count,
+            bytes_accessed=20 * 1024 * 1024,
+            transcendentals=0,
+        ),
+    )(hi, lo, col_hi, col_lo, trailing)
 
 
 def local(diag_block, panel_cols, trailing, geno_top, geno_rest, pheno_top, pheno_rest):
@@ -378,33 +530,29 @@
     rows_piece = panel_cols.shape[0]
     row_count = rows_piece * pcol_size
     variants = geno_top.shape[1]
-    pad = jnp.broadcast_to(pheno_top[:, None], (height, BLOCK))
-    top_aug = jnp.concatenate([geno_top, pad], axis=1)
-    inverse, whole, col_raw, top_all = gather_and_invert(
-        diag_block, top_aug, panel_cols, prow_size, pcol_size
+    inverse, whole, col_raw, top_all, pheno_all = gather_and_invert(
+        diag_block, geno_top, pheno_top.reshape(1, height), panel_cols, prow_size, pcol_size
     )
-    whole = whole.reshape(row_count, width)
-    col_raw = col_raw.reshape(-1, width)
-    top_all = top_all.reshape(width, variants + BLOCK)
-    white_aug = dot3(inverse, top_all, ((1,), (0,)))
-    panel_rows = dot3(whole, inverse, ((1,), (1,)))
-    col_panel = dot3(col_raw, inverse, ((1,), (1,)))
-    own_factor = lax.dynamic_slice_in_dim(
-        panel_rows, lax.axis_index("pcol") * rows_piece, rows_piece, 0
+    hi, lo, col_hi, col_lo, own_factor, white_geno, stats = whiten(
+        inverse,
+        top_all.reshape(width, variants),
+        pheno_all.reshape(1, width),
+        whole.reshape(row_count, width),
+        col_raw.reshape(-1, width),
+        geno_rest,
+        pheno_rest,
+        rows_piece,
     )
-    top_white, pheno_white_top = white_aug[:, :variants], white_aug[:, variants]
-    shift = dot3(panel_rows, white_aug, ((1,), (0,)))
-    white_geno = geno_rest - shift[:, :variants]
-    pheno_white = pheno_rest - shift[:, variants]
-    part_score = jnp.dot(pheno_white, white_geno, precision=HIGHEST)
-    part_info = jnp.sum(white_geno * white_geno, axis=0)
-    score_sum, info_sum = lax.psum((part_score, part_info), "prow")
-    updated_block = trailing - dot3(panel_rows, col_panel, ((1,), (1,)))
-    count = width + row_count * prow_size
-    score_stat = (score_sum + jnp.dot(pheno_white_top, top_white, precision=HIGHEST)) / jnp.sqrt(
-        jnp.float32(count)
-    )
-    info_stat = (info_sum + jnp.sum(top_white * top_white, axis=0)) / jnp.float32(count)
+
+    def fetch(flip):
+        return lax.ppermute(stats, "prow", [(i, i ^ flip) for i in range(prow_size)])
+
+    sib, cross, diag = fetch(1), fetch(2), fetch(3)
+    updated_block = update(hi, lo, col_hi, col_lo, trailing)
+    total = (stats + sib) + (cross + diag)
+    count = jnp.float32(width + row_count * prow_size)
+    score_stat = (total[0] + stats[2]) / jnp.sqrt(count)
+    info_stat = (total[1] + stats[3]) / count
     return (updated_block, own_factor, white_geno, score_stat, info_stat)
 
 

time: 120 us -> 137 us (1.14)
  the two profiles are of different devices: /device:TPU:18 before, /device:TPU:7 now
where the time goes in v1:
time: 137 us; the launch traced here: 135 us
  Pallas kernels  99.3 us (72%)
  starting transfers between devices  28 us (20%)
  local copies, waits for them, and re-layouts  6.82 us (5%)
    pallas_call x1, Pallas kernels, gather_and_invert(): pl.pallas_call(functools.partial(gather_kernel, ly, lz, pcol_size // prow...  69.6 us
    ppermute x3, starting transfers between devices, fetch(): lax.ppermute(stats, 'prow', [(i, i ^ flip) for i in range(prow_size)])  28 us
    pallas_call x1, Pallas kernels, whiten(): pl.pallas_call(functools.partial(whiten_kernel, tile, rows_piece, col_til...  17.4 us
    pallas_call x1, Pallas kernels, update(): pl.pallas_call(update_kernel, grid=(row_count // tile,), in_specs=[left,...  12.3 us
    unnamed x12, local copies, waits for them, and re-layouts  6.82 us
  transfers between devices with their start and end apart: 3, of which 0 were waited for; matrix products, arithmetic and copies ran while one was open for 0% of the time, Pallas kernels for 9%

profile of v1, /device:TPU:7, one launch (start us, length us, event | category | flops | bytes accessed | tf_op | source)
XLA Modules:
  0.0 135.4 jit_solution(1331367259127356302)
XLA Ops:
  0.6 69.6 %shard_map.110 = (f32[512,512]{1,0:T(8,128)}, f32[8,256,512]{2,1,0:T(8,128)}, f32[4,256,512]{2,1,0:T(8,128)}, f32[4,128,256]{2,1,0:T(8,128)}, f32[4,1,128]{2,1,0:T(1,128)}) custom-call(f32[128,512]{1,0:T(8,128)} %diag_in.1, f32[128,256]{1,0:T(8,128)} %top_in.1, f32[1,128]{1,0:T(1,128)} %bitcast.14, f32[256,512]{1,0:T(8,128)} %panel_in.1), custom_call_target="tpu_custom_call" | custom-call | tf_op jit(solution)/shard_map/pallas_call | solution.py:351
  70.2 0.0 copy-start
  70.2 1.6 %copy-done = f32[2048,256]{1,0:T(8,128)S(1)} copy-done((f32[2048,256]{1,0:T(8,128)S(1)}, f32[2048,256]{1,0:T(8,128)}, u32[]{:S(2)}) %copy-start) | copy-done | bytes 2097176
  71.8 0.0 copy-start.1
  71.8 1.6 %copy-done.1 = f32[4,256,512]{2,1,0:T(8,128)S(1)} copy-done((f32[4,256,512]{2,1,0:T(8,128)S(1)}, f32[4,256,512]{2,1,0:T(8,128)}, u32[]{:S(2)}) %copy-start.1) | copy-done | bytes 2097176
  73.4 0.0 copy-start.2
  73.4 1.2 copy-done.2
  74.6 0.0 copy-start.3
  74.6 1.0 copy-done.3
  75.7 0.0 copy-start.4
  75.7 0.7 copy-done.4
  76.4 0.0 copy-start.5
  76.4 0.7 copy-done.5
  77.1 17.4 %shard_map.111 = (bf16[2048,512]{1,0:T(8,128)(2,1)S(1)}, bf16[2048,512]{1,0:T(8,128)(2,1)S(1)}, bf16[512,1024]{1,0:T(8,128)(2,1)S(1)}, bf16[512,1024]{1,0:T(8,12...) custom-call(f32[512,512]{1,0:T(8,128)S(1)} %copy-done.2, f32[512,256]{1,0:T(8,128)S(1)} %bitcast.9, ...), custom_call_target="tpu_custom_call" | custom-call | flops 4831838208 | bytes 16777216 | tf_op jit(solution)/shard_map/pallas_call | solution.py:457
  94.5 27.6 %collective-permute-start.2 = (f32[8,256]{1,0:T(8,128)S(1)}, f32[8,256]{1,0:T(8,128)S(1)}, u32[]{:S(2)}, u32[]{:S(2)}) collective-permute-start(f32[8,256]{1,0:T(8,128)S(1)} %get-tuple-element.28), channel_id=1, source_target_pairs={{0,24},{8,16},{16,8},{24,0},{1,25},{9,17},{17,9},{25,1},{2,26},{10... | collective-permute-start | bytes 24584 | tf_op jit(solution)/shard_map/ppermute | solution.py:548
  122.0 0.0 collective-permute-start.1
  122.1 0.4 collective-permute-start
  122.5 12.3 %shard_map.112 = f32[2048,1024]{1,0:T(8,128)} custom-call(bf16[2048,512]{1,0:T(8,128)(2,1)S(1)} %get-tuple-element.22.hi_in, bf16[2048,512]{1,0:T(8,128)(2,1)S(1)} %get-tuple-element.23.lo_in, bf16[512,1024]{1,0:T(8,128)(2,1)S(1)} %get-tuple-element.24.col_hi_in, bf16[512,1024]{1,0:T(8,128)(2,1)S(1)} %get-tuple-element.25.col_lo_in, f32[2048,1024]{1,0:T(8,128)} %trailing_in.1), custom_call_target="tpu_custom_call" | custom-call | flops 6442450944 | bytes 20971520 | tf_op jit(solution)/shard_map/pallas_call | solution.py:512
  134.8 0.0 collective-permute-done.2
  134.8 0.0 collective-permute-done.1
  134.8 0.0 collective-permute-done
  134.8 0.6 fusion
  (1 shorter events, 0.0 us)
Async XLA Ops:
  70.2 1.6 %copy-start = (f32[2048,256]{1,0:T(8,128)S(1)}, f32[2048,256]{1,0:T(8,128)}, u32[]{:S(2)}) copy-start(f32[2048,256]{1,0:T(8,128)} %geno_in.1) | copy-start | bytes 6291460
  71.8 1.6 %copy-start.1 = (f32[4,256,512]{2,1,0:T(8,128)S(1)}, f32[4,256,512]{2,1,0:T(8,128)}, u32[]{:S(2)}) copy-start(f32[4,256,512]{2,1,0:T(8,128)} %get-tuple-element.21) | copy-start | bytes 6291460
  73.4 1.2 copy-start.2
  74.6 1.0 copy-start.3
  75.7 0.7 copy-start.4
  76.4 0.7 copy-start.5
  94.5 40.3 %collective-permute-start.2 = (f32[8,256]{1,0:T(8,128)S(1)}, f32[8,256]{1,0:T(8,128)S(1)}, u32[]{:S(2)}, u32[]{:S(2)}) collective-permute-start(f32[8,256]{1,0:T(8,128)S(1)} %get-tuple-element.28), channel_id=1, source_target_pairs={{0,24},{8,16},{16,8},{24,0},{1,25},{9,17},{17,9},{25,1},{2,26},{10... | collective-permute-start | bytes 24584 | tf_op jit(solution)/shard_map/ppermute | solution.py:548
  122.0 12.7 %collective-permute-start.1 = (f32[8,256]{1,0:T(8,128)S(1)}, f32[8,256]{1,0:T(8,128)S(1)}, u32[]{:S(2)}, u32[]{:S(2)}) collective-permute-start(f32[8,256]{1,0:T(8,128)S(1)} %get-tuple-element.28), channel_id=1, source_target_pairs={{0,16},{8,24},{16,0},{24,8},{1,17},{9,25},{17,1},{25,9},{2,18},{10... | collective-permute-start | bytes 24584 | tf_op jit(solution)/shard_map/ppermute | solution.py:548
  122.1 12.7 %collective-permute-start = (f32[8,256]{1,0:T(8,128)S(1)}, f32[8,256]{1,0:T(8,128)S(1)}, u32[]{:S(2)}, u32[]{:S(2)}) collective-permute-start(f32[8,256]{1,0:T(8,128)S(1)} %get-tuple-element.28), channel_id=1, source_target_pairs={{0,8},{8,0},{16,24},{24,16},{1,9},{9,1},{17,25},{25,17},{2,10},{10... | collective-permute-start | bytes 24584 | tf_op jit(solution)/shard_map/ppermute | solution.py:548

commit v2 on v1

--- a/solution.py
+++ b/solution.py
@@ -9,7 +9,8 @@
 
 MESH = pl.DeviceIdType.MESH
 HIGHEST = lax.Precision.HIGHEST
-TILE = 8
+TILE = 16
+PARTS = 4
 BLOCK = 128
 
 
@@ -28,19 +29,23 @@
     cols = [jnp.broadcast_to(rolled[:, k : k + 1], (TILE, BLOCK)) for k in range(TILE)]
     rows = lax.broadcasted_iota(jnp.int32, (TILE, BLOCK), 0)
     lanes = lax.broadcasted_iota(jnp.int32, (TILE, BLOCK), 1)
+    pivots = jnp.zeros_like(left)
     for j in range(TILE):
         pivot = jnp.broadcast_to(cols[j][j : j + 1, :], (TILE, BLOCK))
-        inv = lax.rsqrt(pivot)
-        inv = inv * (1.5 - (0.5 * pivot) * inv * inv)
-        factor = jnp.where(rows > j, cols[j] * inv, 0.0)
+        inv = pl.reciprocal(pivot, approx=True)
+        inv = inv * (2.0 - pivot * inv)
+        below = jnp.where(rows > j, cols[j], 0.0)
+        pivots = jnp.where(rows == j, pivot, pivots)
 
         def work(value):
-            scaled = jnp.broadcast_to(value[j : j + 1, :], (TILE, BLOCK)) * inv
-            return jnp.where(rows == j, scaled, value - factor * scaled)
-
-        left, right = work(left), work(right)
+            return value - below * (jnp.broadcast_to(value[j : j + 1, :], (TILE, BLOCK)) * inv)
+
         for k in range(j + 1, TILE):
             cols[k] = work(cols[k])
+        left, right = work(left), work(right)
+    scale = lax.rsqrt(pivots)
+    scale = scale * (1.5 - (0.5 * pivots) * scale * scale)
+    left, right = left * scale, right * scale
     m_ref[pl.ds(start, TILE), :BLOCK] = left
     m_ref[pl.ds(start, TILE), BLOCK:] = right
     both = jnp.concatenate([left, right], axis=1)
@@ -78,14 +83,14 @@
         lo, hi = k * BLOCK, (k + 1) * BLOCK
         m_ref[:, :BLOCK] = a_ref[lo:hi, lo:hi]
         m_ref[:, BLOCK:] = eye
-        for part in range(2):
+        for part in range(PARTS):
 
             def body(step, carry):
                 tile_step(m_ref, step)
                 return carry
 
-            lax.fori_loop(part * tiles // 2, (part + 1) * tiles // 2, body, 0)
-            if part == 0:
+            lax.fori_loop(part * tiles // PARTS, (part + 1) * tiles // PARTS, body, 0)
+            if part < PARTS - 1:
                 if slot < len(events):
                     events[slot]()
                 slot += 1
@@ -269,23 +274,20 @@
             small_wait(kind, cross)
             small(kind, 2).start()
 
-    def first_event():
-        hop(1)
-        across(0)
-
-    def make(d):
-        def run():
-            if d < lz:
-                hop(d)
-            across(d - 1)
-
-        return run
-
     def nothing():
         pass
 
-    events = [first_event, top_event, make(2), nothing, make(3), nothing, nothing]
-    events += [make(d) for d in range(4, lz + 1)]
+    def hop_at(d):
+        return functools.partial(hop, d) if d < lz else nothing
+
+    def across_at(d):
+        return functools.partial(across, d) if d < lz else nothing
+
+    events = [hop_at(1), across_at(0), top_event, nothing, hop_at(2), nothing, nothing, nothing]
+    events += [hop_at(3), across_at(1), nothing, nothing, across_at(2), nothing, nothing, nothing]
+    for d in range(4, lz):
+        events += [hop_at(d), across_at(d - 1)]
+    events.append(across_at(lz - 1))
     invert(a_ref, w_out, m_ref, events)
 
     def handed(i):
@@ -357,7 +359,7 @@
             jax.ShapeDtypeStruct((prow_size,) + geno_top.shape, f32),
             jax.ShapeDtypeStruct((prow_size,) + pheno_row.shape, f32),
         ),
-        in_specs=[any_spec] * 4,
+        in_specs=[pl.BlockSpec(memory_space=pltpu.HBM)] * 4,
         out_specs=(vmem, any_spec, any_spec, any_spec, any_spec),
         scratch_shapes=[
             pltpu.VMEM((width, width), f32),
@@ -371,7 +373,7 @@
             dma((4 + col_parts,)),
         ],
         compiler_params=pltpu.CompilerParams(
-            collective_id=0, has_side_effects=True, vmem_limit_bytes=56 * 1024 * 1024
+            collective_id=0, has_side_effects=True, vmem_limit_bytes=24 * 1024 * 1024
         ),
     )(diag_block, geno_top, pheno_row, panel_cols)
 
@@ -386,10 +388,9 @@
 
 
 def dot3(a, b, dims):
-    def one(x, y):
-        return lax.dot_general(x, y, (dims, ((), ())), preferred_element_type=jnp.float32)
-
-    return one(a[0], b[0]) + (one(a[0], b[1]) + one(a[1], b[0]))
+    left = jnp.concatenate([a[0], a[0], a[1]], axis=dims[0][0])
+    right = jnp.concatenate([b[0], b[1], b[0]], axis=dims[1][0])
+    return lax.dot_general(left, right, (dims, ((), ())), preferred_element_type=jnp.float32)
 
 
 def whiten_kernel(
@@ -488,7 +489,7 @@
             pltpu.VMEM((16, width), bf16),
             pltpu.VMEM((tile, width), f32),
         ],
-        compiler_params=pltpu.CompilerParams(vmem_limit_bytes=40 * 1024 * 1024),
+        compiler_params=pltpu.CompilerParams(vmem_limit_bytes=20 * 1024 * 1024),
         cost_estimate=pl.CostEstimate(
             flops=6 * width * width * (row_count + col_count),
             bytes_accessed=16 * 1024 * 1024,
@@ -515,7 +516,7 @@
         in_specs=[left, left, right, right, block],
         out_specs=block,
         out_shape=jax.ShapeDtypeStruct(trailing.shape, jnp.float32),
-        compiler_params=pltpu.CompilerParams(vmem_limit_bytes=40 * 1024 * 1024),
+        compiler_params=pltpu.CompilerParams(vmem_limit_bytes=20 * 1024 * 1024),
         cost_estimate=pl.CostEstimate(
             flops=6 * width * row_count * col_count,
             bytes_accessed=20 * 1024 * 1024,

time: 137 us -> 96.9 us (0.71)
  starting transfers between devices: 28 us -> 2.14 us
  Pallas kernels: 99.3 us -> 87.4 us
    ppermute x3, starting transfers between devices: 28 us -> 2.14 us  [fetch(): lax.ppermute(stats, 'prow', [(i, i ^ flip) for i in range(prow_size)])]
    pallas_call x1, Pallas kernels: 69.6 us -> 61.9 us  [gather_and_invert(): pl.pallas_call(functools.partial(gather_kernel, ly, lz, pcol_size // prow...]
    pallas_call x1, Pallas kernels: 12.3 us -> 9.1 us  [update(): pl.pallas_call(update_kernel, grid=(row_count // tile,), in_specs=[left,...]
    unnamed x12 -> x16, local copies, waits for them, and re-layouts: 6.82 us -> 5.83 us
where the time goes in v2:
time: 96.9 us; the launch traced here: 96.6 us
  Pallas kernels  87.4 us (90%)
  local copies, waits for them, and re-layouts  5.83 us (6%)
  starting transfers between devices  2.14 us (2%)
    pallas_call x1, Pallas kernels, gather_and_invert(): pl.pallas_call(functools.partial(gather_kernel, ly, lz, pcol_size // prow...  61.9 us
    pallas_call x1, Pallas kernels, whiten(): pl.pallas_call(functools.partial(whiten_kernel, tile, rows_piece, col_til...  16.4 us
    pallas_call x1, Pallas kernels, update(): pl.pallas_call(update_kernel, grid=(row_count // tile,), in_specs=[left,...  9.1 us
    unnamed x16, local copies, waits for them, and re-layouts  5.83 us
    ppermute x3, starting transfers between devices, fetch(): lax.ppermute(stats, 'prow', [(i, i ^ flip) for i in range(prow_size)])  2.14 us
  transfers between devices with their start and end apart: 3, of which 0 were waited for; matrix products, arithmetic and copies ran while one was open for 0% of the time, Pallas kernels for 9%

profile of v2, /device:TPU:7, one launch (start us, length us, event | category | flops | bytes accessed | tf_op | source)
XLA Modules:
  0.0 96.6 jit_solution(540889018813371805)
XLA Ops:
  0.6 0.0 copy-start
  0.6 1.0 %copy-done = f32[256,512]{1,0:T(8,128)S(1)} copy-done((f32[256,512]{1,0:T(8,128)S(1)}, f32[256,512]{1,0:T(8,128)}, u32[]{:S(2)}) %copy-start) | copy-done | bytes 524312
  1.7 0.0 copy-start.1
  1.7 0.9 copy-done.1
  2.6 0.0 copy-start.2
  2.6 0.9 copy-done.2
  3.5 0.0 copy-start.3
  3.5 0.7 copy-done.3
  4.2 0.0 slice-start
  4.2 61.9 %shard_map.110 = (f32[512,512]{1,0:T(8,128)S(1)}, f32[8,256,512]{2,1,0:T(8,128)S(1)}, f32[4,256,512]{2,1,0:T(8,128)S(1)}, f32[4,128,256]{2,1,0:T(8,128)S(1)}, f32[4,1,128]{2,1,0:T(1,128)S(1)}) custom-call(f32[128,512]{1,0:T(8,128)S(1)} %copy-done.1, f32[128,256]{1,0:T(8,128)S(1)} %copy-done.2, f32[1,128]{1,0:T(1,128)S(1)} %bitcast.8, f32[256,512]{1,0:T(8,128)S(1)} %copy-done), custom_call_target="tpu_custom_call" | custom-call | tf_op jit(solution)/shard_map/pallas_call | solution.py:353
  66.1 0.0 copy-start.4
  66.1 1.6 %copy-done.4 = f32[2048,256]{1,0:T(8,128)S(1)} copy-done((f32[2048,256]{1,0:T(8,128)S(1)}, f32[2048,256]{1,0:T(8,128)}, u32[]{:S(2)}) %copy-start.4) | copy-done | bytes 2097176
  67.7 0.0 copy-start.5
  67.7 0.7 copy-done.5
  68.4 0.0 slice-start.1
  68.4 16.4 %shard_map.111 = (bf16[2048,512]{1,0:T(8,128)(2,1)S(1)}, bf16[2048,512]{1,0:T(8,128)(2,1)S(1)}, bf16[512,1024]{1,0:T(8,128)(2,1)S(1)}, bf16[512,1024]{1,0:T(8,12...) custom-call(f32[512,512]{1,0:T(8,128)S(1)} %get-tuple-element.17.w_in, ...), custom_call_target="tpu_custom_call" | custom-call | flops 4831838208 | bytes 16777216 | tf_op jit(solution)/shard_map/pallas_call | solution.py:458
  84.8 0.0 collective-permute-start.2
  84.8 1.5 %collective-permute-start.1 = (f32[8,256]{1,0:T(8,128)S(1)}, f32[8,256]{1,0:T(8,128)S(1)}, u32[]{:S(2)}, u32[]{:S(2)}) collective-permute-start(f32[8,256]{1,0:T(8,128)S(1)} %get-tuple-element.28), channel_id=1, source_target_pairs={{0,16},{8,24},{16,0},{24,8},{1,17},{9,25},{17,1},{25,9},{2,18},{10... | collective-permute-start | bytes 24584 | tf_op jit(solution)/shard_map/ppermute | solution.py:549
  86.3 0.6 collective-permute-start
  86.9 0.0 slice-done
  86.9 0.0 slice-done.1
  86.9 9.1 %shard_map.112 = f32[2048,1024]{1,0:T(8,128)} custom-call(bf16[2048,512]{1,0:T(8,128)(2,1)S(1)} %get-tuple-element.22.hi_in, bf16[2048,512]{1,0:T(8,128)(2,1)S(1)} %get-tuple-element.23.lo_in, bf16[512,1024]{1,0:T(8,128)(2,1)S(1)} %get-tuple-element.24.col_hi_in, bf16[512,1024]{1,0:T(8,128)(2,1)S(1)} %get-tuple-element.25.col_lo_in, f32[2048,1024]{1,0:T(8,128)S(1)} %bitcast.10), custom_call_target="tpu_custom_call" | custom-call | flops 6442450944 | bytes 20971520 | tf_op jit(solution)/shard_map/pallas_call | solution.py:513
  96.0 0.0 collective-permute-done.2
  96.0 0.0 collective-permute-done.1
  96.0 0.0 collective-permute-done
  96.0 0.6 fusion
  (2 shorter events, 0.0 us)
Async XLA Ops:
  0.6 1.0 %copy-start = (f32[256,512]{1,0:T(8,128)S(1)}, f32[256,512]{1,0:T(8,128)}, u32[]{:S(2)}) copy-start(f32[256,512]{1,0:T(8,128)} %panel_in.1) | copy-start | bytes 1572868
  1.7 0.9 copy-start.1
  2.6 0.9 copy-start.2
  3.5 0.7 copy-start.3
  4.2 82.7 %slice-start = ((s8[8388608]{0:T(1024)(128)(4,1)}), s8[4194304]{0:T(1024)(128)(4,1)S(1)}, s32[]{:S(2)}) async-start(s8[8388608]{0:T(1024)(128)(4,1)} %bitcast.9), calls=%async_computation | async-start | bytes 8388608
  66.1 1.6 %copy-start.4 = (f32[2048,256]{1,0:T(8,128)S(1)}, f32[2048,256]{1,0:T(8,128)}, u32[]{:S(2)}) copy-start(f32[2048,256]{1,0:T(8,128)} %geno_in.1) | copy-start | bytes 6291460
  67.7 0.7 copy-start.5
  68.4 18.6 %slice-start.1 = ((s8[8388608]{0:T(1024)(128)(4,1)}), s8[4194304]{0:T(1024)(128)(4,1)S(1)}, s32[]{:S(2)}) async-start(s8[8388608]{0:T(1024)(128)(4,1)} %bitcast.9), calls=%async_computation.1 | async-start | bytes 8388608
  84.8 11.2 %collective-permute-start.2 = (f32[8,256]{1,0:T(8,128)S(1)}, f32[8,256]{1,0:T(8,128)S(1)}, u32[]{:S(2)}, u32[]{:S(2)}) collective-permute-start(f32[8,256]{1,0:T(8,128)S(1)} %get-tuple-element.28), channel_id=1, source_target_pairs={{0,24},{8,16},{16,8},{24,0},{1,25},{9,17},{17,9},{25,1},{2,26},{10... | collective-permute-start | bytes 24584 | tf_op jit(solution)/shard_map/ppermute | solution.py:549
  84.8 11.2 %collective-permute-start.1 = (f32[8,256]{1,0:T(8,128)S(1)}, f32[8,256]{1,0:T(8,128)S(1)}, u32[]{:S(2)}, u32[]{:S(2)}) collective-permute-start(f32[8,256]{1,0:T(8,128)S(1)} %get-tuple-element.28), channel_id=1, source_target_pairs={{0,16},{8,24},{16,0},{24,8},{1,17},{9,25},{17,1},{25,9},{2,18},{10... | collective-permute-start | bytes 24584 | tf_op jit(solution)/shard_map/ppermute | solution.py:549
  86.3 9.7 %collective-permute-start = (f32[8,256]{1,0:T(8,128)S(1)}, f32[8,256]{1,0:T(8,128)S(1)}, u32[]{:S(2)}, u32[]{:S(2)}) collective-permute-start(f32[8,256]{1,0:T(8,128)S(1)} %get-tuple-element.28), channel_id=1, source_target_pairs={{0,8},{8,0},{16,24},{24,16},{1,9},{9,1},{17,25},{25,17},{2,10},{10... | collective-permute-start | bytes 24584 | tf_op jit(solution)/shard_map/ppermute | solution.py:549

commit v3 on v2

--- a/solution.py
+++ b/solution.py
@@ -284,7 +284,7 @@
         return functools.partial(across, d) if d < lz else nothing
 
     events = [hop_at(1), across_at(0), top_event, nothing, hop_at(2), nothing, nothing, nothing]
-    events += [hop_at(3), across_at(1), nothing, nothing, across_at(2), nothing, nothing, nothing]
+    events += [nothing, across_at(1), hop_at(3), nothing, nothing, across_at(2), nothing, nothing]
     for d in range(4, lz):
         events += [hop_at(d), across_at(d - 1)]
     events.append(across_at(lz - 1))
@@ -393,30 +393,40 @@
     return lax.dot_general(left, right, (dims, ((), ())), preferred_element_type=jnp.float32)
 
 
+def column(row):
+    return jnp.transpose(jnp.broadcast_to(row, (BLOCK, row.shape[1])))
+
+
+def weighted(weights, values):
+    wide = jnp.concatenate([weights] * (values.shape[1] // BLOCK), axis=1)
+    return jnp.sum(wide * values, axis=0, keepdims=True)
+
+
 def whiten_kernel(
     tile, pieces, col_tiles,
     w_in, top_in, pheno_in, rows_in, cols_in, geno_in, rest_in,
     hi_out, lo_out, col_hi_out, col_lo_out, own_out, geno_out, stat_out,
-    w_hi, w_lo, top_hi, top_lo, pheno_hi, pheno_lo, kept,
+    w_hi, w_lo, turned_hi, turned_lo, top_hi, top_lo, kept,
 ):
     step = pl.program_id(0)
     place = lax.axis_index("pcol") * own_out.shape[0]
+    variants = geno_in.shape[1]
 
     @pl.when(step == 0)
     def _():
         w_hi[...], w_lo[...] = split2(w_in[...])
         w = (w_hi[...], w_lo[...])
-        white = dot3(w, split2(top_in[...]), INNER)
-        top_hi[...], top_lo[...] = split2(white)
-        row = jnp.broadcast_to(pheno_in[...], pheno_hi.shape)
-        pheno = split2(dot3(split2(row), w, LAST))
-        pheno_hi[...], pheno_lo[...] = pheno
+        turned_hi[...], turned_lo[...] = split2(jnp.transpose(w_in[...]))
+        joined = jnp.concatenate([top_in[...], column(pheno_in[...])], axis=1)
+        both = dot3(w, split2(joined), INNER)
+        top_hi[...], top_lo[...] = split2(both)
+        white = both[:, :variants]
         stat_out[...] = jnp.zeros_like(stat_out)
-        stat_out[2:3, :] = dot3(pheno, (top_hi[...], top_lo[...]), INNER)[:1]
+        stat_out[2:3, :] = weighted(both[:, variants:], white)
         stat_out[3:4, :] = jnp.sum(white * white, axis=0, keepdims=True)
 
     w = (w_hi[...], w_lo[...])
-    panel = dot3(split2(rows_in[...]), w, LAST)
+    panel = dot3(split2(rows_in[...]), (turned_hi[...], turned_lo[...]), INNER)
     parts = split2(panel)
     hi_out[...], lo_out[...] = parts
 
@@ -430,10 +440,10 @@
     def _():
         col_hi_out[...], col_lo_out[...] = split2(dot3(w, split2(cols_in[...]), LAST))
 
-    white = geno_in[...] - dot3(parts, (top_hi[...], top_lo[...]), INNER)
+    shift = dot3(parts, (top_hi[...], top_lo[...]), INNER)
+    white = geno_in[...] - shift[:, :variants]
     geno_out[...] = white
-    pheno = rest_in[0] - dot3((pheno_hi[...], pheno_lo[...]), parts, LAST)
-    stat_out[0:1, :] += dot3(split2(pheno), split2(white), INNER)[:1]
+    stat_out[0:1, :] += weighted(column(rest_in[0]) - shift[:, variants:], white)
     stat_out[1:2, :] += jnp.sum(white * white, axis=0, keepdims=True)
 
 
@@ -483,10 +493,10 @@
         scratch_shapes=[
             pltpu.VMEM((width, width), bf16),
             pltpu.VMEM((width, width), bf16),
-            pltpu.VMEM((width, variants), bf16),
-            pltpu.VMEM((width, variants), bf16),
-            pltpu.VMEM((16, width), bf16),
-            pltpu.VMEM((16, width), bf16),
+            pltpu.VMEM((width, width), bf16),
+            pltpu.VMEM((width, width), bf16),
+            pltpu.VMEM((width, variants + BLOCK), bf16),
+            pltpu.VMEM((width, variants + BLOCK), bf16),
             pltpu.VMEM((tile, width), f32),
         ],
         compiler_params=pltpu.CompilerParams(vmem_limit_bytes=20 * 1024 * 1024),

time: 96.9 us -> 95.8 us (0.989)
  Pallas kernels: 87.4 us -> 86.3 us
    pallas_call x1, Pallas kernels: 16.4 us -> 15.3 us  [whiten(): pl.pallas_call(functools.partial(whiten_kernel, tile, rows_piece, col_til...]
  transfers between devices with their start and end apart: 3 -> 3, of which waited for: 0 -> 0; matrix products, arithmetic and copies ran while one was open for 0% -> 0% of each run, Pallas kernels for 9% -> 10%
where the time goes in v3:
time: 95.8 us; the launch traced here: 95.5 us
  Pallas kernels  86.3 us (90%)
  local copies, waits for them, and re-layouts  5.83 us (6%)
  starting transfers between devices  2.14 us (2%)
    pallas_call x1, Pallas kernels, gather_and_invert(): pl.pallas_call(functools.partial(gather_kernel, ly, lz, pcol_size // prow...  61.9 us
    pallas_call x1, Pallas kernels, whiten(): pl.pallas_call(functools.partial(whiten_kernel, tile, rows_piece, col_til...  15.3 us
    pallas_call x1, Pallas kernels, update(): pl.pallas_call(update_kernel, grid=(row_count // tile,), in_specs=[left,...  9.09 us
    unnamed x16, local copies, waits for them, and re-layouts  5.83 us
    ppermute x3, starting transfers between devices, fetch(): lax.ppermute(stats, 'prow', [(i, i ^ flip) for i in range(prow_size)])  2.14 us
  transfers between devices with their start and end apart: 3, of which 0 were waited for; matrix products, arithmetic and copies ran while one was open for 0% of the time, Pallas kernels for 10%

profile of v3, /device:TPU:7, one launch (start us, length us, event | category | flops | bytes accessed | tf_op | source)
XLA Modules:
  0.0 95.5 jit_solution(5535047209147485731)
XLA Ops:
  0.6 0.0 copy-start
  0.6 1.0 %copy-done = f32[256,512]{1,0:T(8,128)S(1)} copy-done((f32[256,512]{1,0:T(8,128)S(1)}, f32[256,512]{1,0:T(8,128)}, u32[]{:S(2)}) %copy-start) | copy-done | bytes 524312
  1.7 0.0 copy-start.1
  1.7 0.9 copy-done.1
  2.6 0.0 copy-start.2
  2.6 0.9 copy-done.2
  3.5 0.0 copy-start.3
  3.5 0.7 copy-done.3
  4.2 0.0 slice-start
  4.2 61.9 %shard_map.110 = (f32[512,512]{1,0:T(8,128)S(1)}, f32[8,256,512]{2,1,0:T(8,128)S(1)}, f32[4,256,512]{2,1,0:T(8,128)S(1)}, f32[4,128,256]{2,1,0:T(8,128)S(1)}, f32[4,1,128]{2,1,0:T(1,128)S(1)}) custom-call(f32[128,512]{1,0:T(8,128)S(1)} %copy-done.1, f32[128,256]{1,0:T(8,128)S(1)} %copy-done.2, f32[1,128]{1,0:T(1,128)S(1)} %bitcast.8, f32[256,512]{1,0:T(8,128)S(1)} %copy-done), custom_call_target="tpu_custom_call" | custom-call | tf_op jit(solution)/shard_map/pallas_call | solution.py:353
  66.1 0.0 copy-start.4
  66.1 1.6 %copy-done.4 = f32[2048,256]{1,0:T(8,128)S(1)} copy-done((f32[2048,256]{1,0:T(8,128)S(1)}, f32[2048,256]{1,0:T(8,128)}, u32[]{:S(2)}) %copy-start.4) | copy-done | bytes 2097176
  67.7 0.0 copy-start.5
  67.7 0.7 copy-done.5
  68.4 0.0 slice-start.1
  68.4 15.3 %shard_map.111 = (bf16[2048,512]{1,0:T(8,128)(2,1)S(1)}, bf16[2048,512]{1,0:T(8,128)(2,1)S(1)}, bf16[512,1024]{1,0:T(8,128)(2,1)S(1)}, bf16[512,1024]{1,0:T(8,12...) custom-call(f32[512,512]{1,0:T(8,128)S(1)} %get-tuple-element.17.w_in, ...), custom_call_target="tpu_custom_call" | custom-call | flops 4831838208 | bytes 16777216 | tf_op jit(solution)/shard_map/pallas_call | solution.py:468
  83.7 0.0 collective-permute-start.2
  83.7 1.5 %collective-permute-start.1 = (f32[8,256]{1,0:T(8,128)S(1)}, f32[8,256]{1,0:T(8,128)S(1)}, u32[]{:S(2)}, u32[]{:S(2)}) collective-permute-start(f32[8,256]{1,0:T(8,128)S(1)} %get-tuple-element.28), channel_id=1, source_target_pairs={{0,16},{8,24},{16,0},{24,8},{1,17},{9,25},{17,1},{25,9},{2,18},{10... | collective-permute-start | bytes 24584 | tf_op jit(solution)/shard_map/ppermute | solution.py:559
  85.2 0.6 collective-permute-start
  85.8 0.0 slice-done
  85.8 0.0 slice-done.1
  85.8 9.1 %shard_map.112 = f32[2048,1024]{1,0:T(8,128)} custom-call(bf16[2048,512]{1,0:T(8,128)(2,1)S(1)} %get-tuple-element.22.hi_in, bf16[2048,512]{1,0:T(8,128)(2,1)S(1)} %get-tuple-element.23.lo_in, bf16[512,1024]{1,0:T(8,128)(2,1)S(1)} %get-tuple-element.24.col_hi_in, bf16[512,1024]{1,0:T(8,128)(2,1)S(1)} %get-tuple-element.25.col_lo_in, f32[2048,1024]{1,0:T(8,128)S(1)} %bitcast.10), custom_call_target="tpu_custom_call" | custom-call | flops 6442450944 | bytes 20971520 | tf_op jit(solution)/shard_map/pallas_call | solution.py:523
  94.9 0.0 collective-permute-done.2
  94.9 0.0 collective-permute-done.1
  94.9 0.0 collective-permute-done
  94.9 0.6 fusion
  (2 shorter events, 0.0 us)
Async XLA Ops:
  0.6 1.0 %copy-start = (f32[256,512]{1,0:T(8,128)S(1)}, f32[256,512]{1,0:T(8,128)}, u32[]{:S(2)}) copy-start(f32[256,512]{1,0:T(8,128)} %panel_in.1) | copy-start | bytes 1572868
  1.7 0.9 copy-start.1
  2.6 0.9 copy-start.2
  3.5 0.7 copy-start.3
  4.2 81.6 %slice-start = ((s8[8388608]{0:T(1024)(128)(4,1)}), s8[4194304]{0:T(1024)(128)(4,1)S(1)}, s32[]{:S(2)}) async-start(s8[8388608]{0:T(1024)(128)(4,1)} %bitcast.9), calls=%async_computation | async-start | bytes 8388608
  66.1 1.6 %copy-start.4 = (f32[2048,256]{1,0:T(8,128)S(1)}, f32[2048,256]{1,0:T(8,128)}, u32[]{:S(2)}) copy-start(f32[2048,256]{1,0:T(8,128)} %geno_in.1) | copy-start | bytes 6291460
  67.7 0.7 copy-start.5
  68.4 17.5 %slice-start.1 = ((s8[8388608]{0:T(1024)(128)(4,1)}), s8[4194304]{0:T(1024)(128)(4,1)S(1)}, s32[]{:S(2)}) async-start(s8[8388608]{0:T(1024)(128)(4,1)} %bitcast.9), calls=%async_computation.1 | async-start | bytes 8388608
  83.7 11.2 %collective-permute-start.2 = (f32[8,256]{1,0:T(8,128)S(1)}, f32[8,256]{1,0:T(8,128)S(1)}, u32[]{:S(2)}, u32[]{:S(2)}) collective-permute-start(f32[8,256]{1,0:T(8,128)S(1)} %get-tuple-element.28), channel_id=1, source_target_pairs={{0,24},{8,16},{16,8},{24,0},{1,25},{9,17},{17,9},{25,1},{2,26},{10... | collective-permute-start | bytes 24584 | tf_op jit(solution)/shard_map/ppermute | solution.py:559
  83.7 11.2 %collective-permute-start.1 = (f32[8,256]{1,0:T(8,128)S(1)}, f32[8,256]{1,0:T(8,128)S(1)}, u32[]{:S(2)}, u32[]{:S(2)}) collective-permute-start(f32[8,256]{1,0:T(8,128)S(1)} %get-tuple-element.28), channel_id=1, source_target_pairs={{0,16},{8,24},{16,0},{24,8},{1,17},{9,25},{17,1},{25,9},{2,18},{10... | collective-permute-start | bytes 24584 | tf_op jit(solution)/shard_map/ppermute | solution.py:559
  85.2 9.7 %collective-permute-start = (f32[8,256]{1,0:T(8,128)S(1)}, f32[8,256]{1,0:T(8,128)S(1)}, u32[]{:S(2)}, u32[]{:S(2)}) collective-permute-start(f32[8,256]{1,0:T(8,128)S(1)} %get-tuple-element.28), channel_id=1, source_target_pairs={{0,8},{8,0},{16,24},{24,16},{1,9},{9,1},{17,25},{25,17},{2,10},{10... | collective-permute-start | bytes 24584 | tf_op jit(solution)/shard_map/ppermute | solution.py:559
